TPU v7x, 32 devices: a whole 2x2x4 slice. The times are simulated.
32 devices in a mesh: col: 8 (over z, x), row: 4 (over y, core).
Axes of the slice: x: 2, y: 2, z: 4, core: 2. Of those that a mesh axis runs over, the one named last changes fastest.
Arguments:
- amp_owned: bfloat16 [9216, 4096], P(('col', 'row')), may hold values from -6 to 6
- pair_of_slot: int32 [9216], replicated, may hold values from 0 to 9215, as said below
- amp_tiles: int32 [72, 32], replicated, may hold values 0 or 1
- integrals: bfloat16 [2, 2048, 8192], P(None, 'row', 'col'), may hold values from -0.09375 to 0.09375
- integral_tile_mask: int32 [2, 16, 64], replicated, may hold values 0 or 1
Outputs:
- ladder: float32 [9216, 8192], P('row', 'col')
Inputs may be any that keep to these rules, and one draw needn't show every extreme that they name: `pair_of_slot`: a permutation of the 9216 occupied pairs; owner slot q lies on the device of index q // 288 along col+row; one owner holds at most 144 pairs of any one grid row (pairs r * 9216 / 4 to (r + 1) * 9216 / 4 - 1), and some owner holds exactly 144 of each grid row.
All inputs are finite; a program needn't handle non-finite values.
Results may differ from a plain program's by a relative error of at most 0.0003.
Values may be sent and summed in bfloat16 or wider, within the bound.
A program may use at most 128 MiB of HBM per device.

v0:
```python
import jax
import jax.numpy as jnp
from jax import lax
from jax.sharding import PartitionSpec as P


def apply_tile_blocks(block_data, tile_map, tile_size):
    row_count, col_count = block_data.shape
    shaped = block_data.reshape(
        row_count // tile_size, tile_size, col_count // tile_size, tile_size
    )
    shaped = shaped * tile_map.astype(block_data.dtype)[:, None, :, None]
    return shaped.reshape(row_count, col_count)


def on_device(amp_owned, pair_of_slot, amp_tiles, integrals, integral_tile_mask):
    n_col = lax.axis_size("col")
    n_row = lax.axis_size("row")
    devices = n_col * n_row
    col_at = lax.axis_index("col")
    row_at = lax.axis_index("row")
    own_rows, width_all = amp_owned.shape
    total_rows = pair_of_slot.shape[0]
    grid_rows = total_rows // n_row
    capacity = 2 * own_rows // n_row
    sections, slab_rows, out_cols = integrals.shape
    slab_width = width_all // sections
    tile_size = total_rows // amp_tiles.shape[0]
    destination = pair_of_slot // grid_rows
    owner_index = jnp.arange(total_rows, dtype=jnp.int32) // own_rows
    onehot = (
        destination.reshape(devices, own_rows)[:, :, None]
        == jnp.arange(n_row, dtype=jnp.int32)[None, None, :]
    ).astype(jnp.int32)
    earlier = jnp.cumsum(onehot, axis=1) - onehot
    slot_rank = jnp.sum(earlier * onehot, axis=2).reshape(total_rows)
    my_index = col_at * n_row + row_at
    my_dest = lax.dynamic_slice_in_dim(destination, my_index * own_rows, own_rows)
    my_rank = lax.dynamic_slice_in_dim(slot_rank, my_index * own_rows, own_rows)
    send_index = (
        jnp.full((n_row * capacity,), own_rows, jnp.int32)
        .at[my_dest * capacity + my_rank]
        .set(jnp.arange(own_rows, dtype=jnp.int32))
    )
    padded = jnp.concatenate([amp_owned, jnp.zeros((1, width_all), jnp.bfloat16)], axis=0)
    chosen = padded[send_index]
    local_row = jnp.where(destination == row_at, pair_of_slot - row_at * grid_rows, grid_rows)
    recv_index = (
        jnp.zeros((grid_rows,), jnp.int32)
        .at[local_row]
        .set(owner_index * capacity + slot_rank, mode="drop")
    )
    row_tiles = grid_rows // tile_size
    my_amp_tiles = lax.dynamic_slice_in_dim(amp_tiles, row_at * row_tiles, row_tiles, 0)
    panels = []
    piece_cols = slab_width // n_col
    dealt_parts = chosen.reshape(n_row, capacity, sections, n_col, piece_cols).transpose(
        3, 0, 1, 2, 4
    )
    arrived = lax.all_to_all(
        dealt_parts.reshape(devices, capacity, sections * piece_cols),
        ("col", "row"),
        split_axis=0,
        concat_axis=0,
        tiled=True,
    )
    amp_grid = arrived.reshape(devices * capacity, sections * piece_cols)[recv_index]
    piece_tiles = piece_cols // tile_size
    for section_part in range(sections):
        tile_cols = lax.dynamic_slice_in_dim(
            my_amp_tiles,
            section_part * (slab_width // tile_size) + col_at * piece_tiles,
            piece_tiles,
            1,
        )
        block_amp = apply_tile_blocks(
            amp_grid[:, section_part * piece_cols : (section_part + 1) * piece_cols],
            tile_cols,
            tile_size,
        )
        panels.append(lax.all_gather(block_amp, "col", axis=1, tiled=True))
    local_tile_rows = slab_rows // tile_size
    col_tiles = out_cols // tile_size
    ladder_sum = jnp.zeros((grid_rows, out_cols), jnp.float32)
    for section_part in range(sections):
        tiles_int = lax.dynamic_slice(
            integral_tile_mask[section_part],
            (row_at * local_tile_rows, col_at * col_tiles),
            (local_tile_rows, col_tiles),
        )
        block_int = apply_tile_blocks(integrals[section_part], tiles_int, tile_size)
        amp_panel = panels[section_part]

        def accumulate(running, piece_int, offset_row, amp_panel=amp_panel):
            return running + jnp.dot(amp_panel, piece_int, preferred_element_type=jnp.float32)

        ladder_sum = accumulate(
            ladder_sum, lax.all_gather(block_int, "row", axis=0, tiled=True), jnp.int32(0)
        )
    return 0.5 * ladder_sum


def solution(mesh):
    placed = (P(("col", "row"), None), P(), P(), P(None, "row", "col"), P())
    return jax.shard_map(
        on_device, mesh=mesh, in_specs=placed, out_specs=P("row", "col"), check_vma=False
    )
```

profile of v0, /device:TPU:24, one launch (start us, length us, event | category | flops | bytes accessed | tf_op | source)
XLA Modules:
  0.0 505.6 jit_solution(2648129515350980254)
XLA Ops:
  6.5 0.8 compare_select_fusion
  7.3 0.1 eq.28
  7.5 3.5 reduce-window.6
  11.0 0.4 slice_reduce_fusion
  11.4 0.1 bitcast_bitcast_fusion
  11.6 0.1 reshape.54
  11.7 2.9 scatter_custom_fusion
  14.7 1.9 concatenate.3
  16.6 5.2 %gather_fusion = bf16[576,4096]{1,0:T(8,128)(2,1)} fusion(bf16[289,4096]{1,0:T(8,128)(2,1)S(1)} %concatenate.3, s32[1024]{0:T(1024)S(1)} %pad_clamp_fusion.1), kind=kCustom, calls=%fused_computation | custom fusion | bytes 9439488 | tf_op jit(solution)/shard_map/gather | solution.py:46
  21.7 6.1 %copy.15 = bf16[72,8,16,256]{3,2,1,0:T(8,128)(2,1)} copy(bf16[72,8,16,256]{3,1,2,0:T(8,128)(2,1)} %bitcast.50) | data formatting | bytes 9437184
  27.8 9.5 %copy.27 = bf16[4,144,2,8,256]{4,2,1,0,3:T(2,128)(2,1)} copy(bf16[4,144,2,8,256]{4,3,2,1,0:T(8,128)(2,1)} %bitcast.48) | data formatting | bytes 9437184 | tf_op jit(solution)/shard_map/reshape | solution.py:57
  37.3 8.6 %reshape.56 = bf16[32,144,512]{2,1,0:T(8,128)(2,1)} reshape(bf16[8,4,144,2,256]{4,3,2,1,0:T(2,128)(2,1)} %bitcast.49) | data formatting | bytes 9437184 | tf_op jit(solution)/shard_map/reshape | solution.py:61
  45.9 5.9 %all-to-all-start = ((bf16[32,144,512]{2,1,0:T(8,128)(2,1)}), bf16[32,144,512]{2,1,0:T(8,128)(2,1)}, u32[]{:S(2)}, u32[]{:S(2)}) async-start(bf16[32,144,512]{2,1,0:T(8,128)(2,1)} %reshape.56), calls=%async_computation | async-start | bytes 9437184 | tf_op jit(solution)/shard_map/all_to_all | solution.py:60
  52.0 0.2 mul.105
  52.2 0.2 mul.111
  52.4 1.7 bitcast_multiply_fusion.2
  54.3 0.8 dynamic-slice_convert_fusion.2
  55.1 0.1 copy.11
  55.2 0.1 copy.12
  55.3 34.4 %scatter_custom_fusion.1 = s32[2304]{0:T(1024)S(1)} fusion(s32[9216]{0:T(1024)S(1)} %get-tuple-element.9, s32[9216]{0:T(1024)S(1)} %fusion.3, s32[]{:T(128)} %constant.73.clone.1), kind=kCustom, calls=%fused_computation.37 | custom fusion | bytes 9220 | tf_op jit(solution)/shard_map/scatter | solution.py:51
  89.7 65.2 %all-to-all-done = bf16[32,144,512]{2,1,0:T(8,128)(2,1)} async-done(((bf16[32,144,512]{2,1,0:T(8,128)(2,1)}), bf16[32,144,512]{2,1,0:T(8,128)(2,1)}, u32[]{:S(2)}, u32[]{:S(2)}) %all-to-all-start) | async-done | bytes 4718624 | tf_op jit(solution)/shard_map/all_to_all | solution.py:60
  155.0 10.0 %gather_fusion.1 = bf16[2304,512]{1,0:T(8,128)(2,1)S(1)} fusion(bf16[4608,512]{1,0:T(8,128)(2,1)} %bitcast.2, s32[3072]{0:T(1024)S(1)} %pad_clamp_fusion), kind=kCustom, calls=%fused_computation.1 | custom fusion | bytes 4727808 | tf_op jit(solution)/shard_map/gather | solution.py:67
  164.9 0.7 mul.100
  165.6 0.7 mul.108
  166.3 1.7 bitcast_multiply_fusion
  168.1 0.7 all-gather.11.cloned.1.call-update
  168.8 0.5 all-gather.9.cloned.1.call-update
  169.4 137.9 %all-gather.5.cloned.1.call-done = bf16[2304,2048]{1,0:T(8,128)(2,1)} async-done(((bf16[2304,256]{1,0:T(8,128)(2,1)}), bf16[2304,2048]{1,0:T(8,128)(2,1)}) %all-gather.5.cloned.1.call-update) | async-done | bytes 9437200 | tf_op jit(solution)/shard_map/all_gather | solution.py:81
  307.3 15.9 %fusion.16 = f32[2304,1024]{1,0:T(8,128)} fusion(bf16[2304,2048]{1,0:T(8,128)(2,1)} %all-gather.5.cloned.1.call-done, bf16[2048,1024]{1,0:T(8,128)(2,1)} %all-gather.7.cloned.1.call-done), kind=kOutput, calls=%fused_computation.51 | convolution fusion | flops 9663676416 | bytes 23068672 | tf_op jit(solution)/shard_map/dot_general | solution.py:95
  323.3 20.2 %all-gather.11.cloned.1.call-done = bf16[2048,1024]{1,0:T(8,128)(2,1)} async-done(((bf16[512,1024]{1,0:T(8,128)(2,1)}), bf16[2048,1024]{1,0:T(8,128)(2,1)}) %all-gather.11.cloned.1.call-update) | async-done | bytes 4194320 | tf_op jit(solution)/shard_map/all_gather | solution.py:98
  343.5 138.2 %all-gather.9.cloned.1.call-done = bf16[2304,2048]{1,0:T(8,128)(2,1)} async-done(((bf16[2304,256]{1,0:T(8,128)(2,1)}), bf16[2304,2048]{1,0:T(8,128)(2,1)}) %all-gather.9.cloned.1.call-update) | async-done | bytes 9437200 | tf_op jit(solution)/shard_map/all_gather | solution.py:81
  481.7 17.3 %add_multiply_fusion = f32[2304,1024]{1,0:T(8,128)} fusion(f32[2304,1024]{1,0:T(8,128)} %fusion.16, bf16[2304,2048]{1,0:T(8,128)(2,1)} %all-gather.9.cloned.1.call-done, bf16[2048,1024]{1,0:T(8,128)(2,1)} %all-gather.11.cloned.1.call-done), kind=kOutput, calls=%fused_computation.4 | convolution fusion | flops 9668395008 | bytes 32505856 | tf_op jit(solution)/shard_map/dot_general | solution.py:95
  (25 shorter events, 0.5 us)
Async XLA Ops:
  45.9 6.0 %copy-start.1 = (s32[2,16,64]{2,1,0:T(8,128)S(1)}, s32[2,16,64]{2,1,0:T(8,128)}, u32[]{:S(2)}) copy-start(s32[2,16,64]{2,1,0:T(8,128)} %param.9) | copy-start | bytes 24580
  45.9 6.5 %copy-start = (bf16[2,512,1024]{2,1,0:T(8,128)(2,1)S(1)}, bf16[2,512,1024]{2,1,0:T(8,128)(2,1)}, u32[]{:S(2)}) copy-start(bf16[2,512,1024]{2,1,0:T(8,128)(2,1)} %param.8) | copy-start | bytes 6291460
  45.9 109.0 %all-to-all-start = ((bf16[32,144,512]{2,1,0:T(8,128)(2,1)}), bf16[32,144,512]{2,1,0:T(8,128)(2,1)}, u32[]{:S(2)}, u32[]{:S(2)}) async-start(bf16[32,144,512]{2,1,0:T(8,128)(2,1)} %reshape.56), calls=%async_computation | async-start | bytes 9437184 | tf_op jit(solution)/shard_map/all_to_all | solution.py:60
  51.9 117.5 %all-gather.7.cloned.1.call-start = ((), (), s32[]{:S(2)}) async-start(), calls=%async_computation.2 | async-start | bytes 5242880 | tf_op jit(solution)/shard_map/all_gather | solution.py:98
  54.2 253.1 %all-gather.5.cloned.1.call-start = ((), (), s32[]{:S(2)}) async-start(), calls=%async_computation.1 | async-start | bytes 10616832 | tf_op jit(solution)/shard_map/all_gather | solution.py:81
  168.0 175.4 %all-gather.11.cloned.1.call-start = ((), (), s32[]{:S(2)}) async-start(), calls=%async_computation.4 | async-start | bytes 5242880 | tf_op jit(solution)/shard_map/all_gather | solution.py:98
  168.8 312.9 %all-gather.9.cloned.1.call-start = ((), (), s32[]{:S(2)}) async-start(), calls=%async_computation.3 | async-start | bytes 10616832 | tf_op jit(solution)/shard_map/all_gather | solution.py:81
Sparse Core Ops, SparseCore 0:
  54.3 66.7 all-gather.6
  168.2 139.1 all-gather.4
  308.9 34.5 all-gather.10
  345.4 136.2 all-gather.8
where the time goes:
time: 510 us; the launch traced here: 506 us
  waiting for transfers between devices  363 us (71%)
  local copies, waits for them, and re-layouts  81.1 us (16%)
  matrix products  33.3 us (7%)
  between operations  13.4 us (3%)
  other arithmetic  8.93 us (2%)
  starting transfers between devices  6.08 us (1%)
    all_gather x2, waiting for transfers between devices, on_device(): panels.append(lax.all_gather(block_amp, 'col', axis=1, tiled=True))  276 us
    all_to_all x1, waiting for transfers between devices, on_device(): lax.all_to_all(dealt_parts.reshape(devices, capacity, sections * piece_co...  65.2 us
    scatter x1, local copies, waits for them, and re-layouts, on_device(): recv_index = jnp.zeros((grid_rows,), jnp.int32).at[local_row].set(owner_i...  34.4 us
    dot_general x2, matrix products, accumulate(): jnp.dot(amp_panel, piece_int, preferred_element_type=jnp.float32)  33.3 us
    all_gather x2, waiting for transfers between devices, on_device(): lax.all_gather(block_int, 'row', axis=0, tiled=True)  20.2 us
  transfers between devices with their start and end apart: 5, of which 4 were waited for; matrix products, arithmetic and copies ran while one was open for 13% of the time, Pallas kernels for 0%

commit v1 on v0

v1 whole, which is shorter than its diff:
```python
import functools

import jax
import jax.numpy as jnp
from jax import lax
from jax.experimental import pallas as pl
from jax.experimental.pallas import tpu as pltpu
from jax.sharding import PartitionSpec as P

MESH = pl.DeviceIdType.MESH


def apply_tile_blocks(block_data, tile_map, tile_size):
    row_count, col_count = block_data.shape
    shaped = block_data.reshape(
        row_count // tile_size, tile_size, col_count // tile_size, tile_size
    )
    shaped = shaped * tile_map.astype(block_data.dtype)[:, None, :, None]
    return shaped.reshape(row_count, col_count)


def spread_kernel(
    lines, width, chunk, a_ref, b_ref, o_ref, full, load, zsend, zrecv, xsend, xrecv
):
    col = lax.axis_index("col")
    z, x = col // width, col % width
    rows = a_ref.shape[0]
    chunks = rows // chunk
    out_cols = o_ref.shape[1]

    barrier = pltpu.get_barrier_semaphore()
    for side in (1, -1):
        near = z + side

        @pl.when((near >= 0) & (near < lines))
        def _(near=near):
            pl.semaphore_signal(
                barrier, inc=1, device_id={"col": near * width + x}, device_id_type=MESH
            )

    for e in range(1, width):
        pl.semaphore_signal(
            barrier, inc=1, device_id={"col": z * width + (x + e) % width}, device_id_type=MESH
        )
    ends = (z == 0).astype(jnp.int32) + (z == lines - 1).astype(jnp.int32)
    pl.semaphore_wait(barrier, width + 1 - ends)

    def along(origin, j, side):
        piece = full.at[origin * width + x, pl.ds(pl.multiple_of(j * chunk, chunk), chunk)]
        return pltpu.make_async_remote_copy(
            src_ref=piece,
            dst_ref=piece,
            send_sem=zsend.at[0 if side > 0 else 1, origin, j],
            recv_sem=zrecv.at[origin, j],
            device_id={"col": (z + side) * width + x},
            device_id_type=MESH,
        )

    def across(origin, j, e, which=None):
        held = x if which is None else which
        piece = full.at[origin * width + held, pl.ds(pl.multiple_of(j * chunk, chunk), chunk)]
        return pltpu.make_async_remote_copy(
            src_ref=piece,
            dst_ref=piece,
            send_sem=xsend.at[e - 1, origin, j],
            recv_sem=xrecv.at[origin * width + held, j],
            device_id={"col": z * width + (x + e) % width},
            device_id_type=MESH,
        )

    def multiply(k, j, first=False):
        at = pl.ds(pl.multiple_of(j * chunk, chunk), chunk)

        def part(n, carry):
            cols = pl.ds(pl.multiple_of(n * 512, 512), 512)
            term = 0.5 * jnp.dot(
                full[k, at, :], b_ref[k, :, cols], preferred_element_type=jnp.float32
            )
            if first:
                o_ref[at, cols] = term
            else:
                o_ref[at, cols] += term
            return carry

        lax.fori_loop(0, out_cols // 512, part, 0)

    own = pltpu.make_async_copy(a_ref, full.at[col], load)
    own.start()
    own.wait()

    def step(t, carry):
        d, j = t // chunks, t % chunks

        @pl.when(d == 0)
        def _():
            for side in (1, -1):

                @pl.when((z + side >= 0) & (z + side < lines))
                def _(side=side):
                    along(z, j, side).start()

            for e in range(1, width):
                across(z, j, e).start()
            multiply(col, j, True)

        for side in (1, -1):
            origin = z - side * d

            @pl.when((d > 0) & (d < lines) & (origin >= 0) & (origin < lines))
            def _(side=side, origin=origin):
                along(origin, j, -side).wait_recv()

                @pl.when((z + side >= 0) & (z + side < lines))
                def _():
                    along(origin, j, side).start()

                for e in range(1, width):
                    across(origin, j, e).start()
                multiply(origin * width + x, j)

        for side in (1, -1):
            origin = z - side * (d - 1)
            due = (d > 0) if side > 0 else (d > 1)

            @pl.when(due & (origin >= 0) & (origin < lines))
            def _(origin=origin):
                for e in range(1, width):
                    there = (x + e) % width
                    across(origin, j, e, there).wait_recv()
                    multiply(origin * width + there, j)

        return carry

    lax.fori_loop(0, (lines + 1) * chunks, step, 0)

    def drain(t, carry):
        origin, j = t // chunks, t % chunks

        @pl.when((origin <= z) & (z < lines - 1))
        def _():
            along(origin, j, 1).wait_send()

        @pl.when((origin >= z) & (z > 0))
        def _():
            along(origin, j, -1).wait_send()

        for e in range(1, width):
            across(origin, j, e).wait_send()
        return carry

    lax.fori_loop(0, lines * chunks, drain, 0)


def spread_multiply(amp_piece, vint, n_col):
    lines = 4 if n_col % 4 == 0 else n_col
    width = n_col // lines
    rows, depth = amp_piece.shape
    out_cols = vint.shape[2]
    chunk = 384 if rows % 384 == 0 else rows
    chunks = rows // chunk
    return pl.pallas_call(
        functools.partial(spread_kernel, lines, width, chunk),
        out_shape=jax.ShapeDtypeStruct((rows, out_cols), jnp.float32),
        in_specs=[
            pl.BlockSpec(memory_space=pl.ANY),
            pl.BlockSpec(memory_space=pltpu.VMEM),
        ],
        out_specs=pl.BlockSpec(memory_space=pltpu.VMEM),
        scratch_shapes=[
            pltpu.VMEM((n_col, rows, depth), jnp.bfloat16),
            pltpu.SemaphoreType.DMA,
            pltpu.SemaphoreType.DMA((2, lines, chunks)),
            pltpu.SemaphoreType.DMA((lines, chunks)),
            pltpu.SemaphoreType.DMA((max(width - 1, 1), lines, chunks)),
            pltpu.SemaphoreType.DMA((n_col, chunks)),
        ],
        compiler_params=pltpu.CompilerParams(
            collective_id=0, has_side_effects=True, vmem_limit_bytes=58 * 1024 * 1024
        ),
        cost_estimate=pl.CostEstimate(
            flops=2 * rows * depth * n_col * out_cols, bytes_accessed=40_000_000, transcendentals=0
        ),
    )(amp_piece, vint)


def on_device(amp_owned, pair_of_slot, amp_tiles, integrals, integral_tile_mask):
    n_col = lax.axis_size("col")
    n_row = lax.axis_size("row")
    col_at = lax.axis_index("col")
    row_at = lax.axis_index("row")
    own_rows, width_all = amp_owned.shape
    total_rows = pair_of_slot.shape[0]
    grid_rows = total_rows // n_row
    sections, slab_rows, out_cols = integrals.shape
    tile_size = total_rows // amp_tiles.shape[0]
    piece_cols = width_all // n_col
    row_tiles = grid_rows // tile_size
    piece_tiles = piece_cols // tile_size

    local_tile_rows = slab_rows // tile_size
    col_tiles = out_cols // tile_size
    tiles_int = lax.dynamic_slice(
        integral_tile_mask,
        (0, row_at * local_tile_rows, col_at * col_tiles),
        (sections, local_tile_rows, col_tiles),
    )
    masked = apply_tile_blocks(
        integrals.reshape(sections * slab_rows, out_cols),
        tiles_int.reshape(sections * local_tile_rows, col_tiles),
        tile_size,
    ).reshape(sections, slab_rows, out_cols)
    vint = lax.all_gather(masked, "row", axis=1, tiled=True)
    vint = vint.reshape(n_col, piece_cols, out_cols)

    dealt = amp_owned.reshape(own_rows, n_col, piece_cols).transpose(1, 0, 2)
    dealt = lax.all_to_all(dealt, "col", split_axis=0, concat_axis=0, tiled=True)
    everyone = lax.all_gather(dealt, "row", axis=0, tiled=False)
    everyone = everyone.reshape(total_rows, piece_cols)

    slot = jnp.arange(total_rows, dtype=jnp.int32)
    owner, within = slot // own_rows, slot % own_rows
    place = ((owner % n_row) * n_col + owner // n_row) * own_rows + within
    high = (
        (pair_of_slot // tile_size - row_at * row_tiles)[:, None]
        == jnp.arange(row_tiles, dtype=jnp.int32)[None, :]
    ).astype(jnp.bfloat16)
    low = (pair_of_slot % tile_size)[:, None] == jnp.arange(tile_size, dtype=jnp.int32)[None, :]
    zero = jnp.zeros((), jnp.bfloat16)
    low = jnp.concatenate(
        [
            jnp.where(low, (place // 128).astype(jnp.bfloat16)[:, None], zero),
            jnp.where(low, (place % 128).astype(jnp.bfloat16)[:, None], zero),
        ],
        axis=1,
    )
    found = lax.dot_general(
        high, low, (((0,), (0,)), ((), ())), preferred_element_type=jnp.float32
    ).astype(jnp.int32)
    found = (found[:, :tile_size] * 128 + found[:, tile_size:]).reshape(grid_rows)

    my_tiles = lax.dynamic_slice(
        amp_tiles, (row_at * row_tiles, col_at * piece_tiles), (row_tiles, piece_tiles)
    )
    amp_piece = apply_tile_blocks(
        everyone.at[found].get(mode="promise_in_bounds"), my_tiles, tile_size
    )
    return spread_multiply(amp_piece, vint, n_col)


def solution(mesh):
    placed = (P(("col", "row"), None), P(), P(), P(None, "row", "col"), P())
    return jax.shard_map(
        on_device, mesh=mesh, in_specs=placed, out_specs=P("row", "col"), check_vma=False
    )
```

time: 510 us -> 428 us (0.84)
  waiting for transfers between devices: 363 us -> 93.1 us
  Pallas kernels: 0 us -> 216 us
  blocking collectives: 0 us -> 57.1 us
  local copies, waits for them, and re-layouts: 81.1 us -> 30 us
  matrix products: 33.3 us -> 0.72 us
  starting transfers between devices: 6.08 us -> 0.04 us
  other arithmetic: 8.93 us -> 14.4 us
    pallas_call x0 -> x1, Pallas kernels: none -> 216 us  [spread_multiply(): pl.pallas_call(functools.partial(spread_kernel, lines, width, chunk), out...]
    all_gather x4 -> x2, waiting for transfers between devices: 296 us -> 93 us  [the longest x1 47.5 us: on_device(): everyone = lax.all_gather(dealt, 'row', axis=0, tiled=False)]
    all_to_all x1 -> x0, waiting for transfers between devices: 65.2 us -> none  [on_device(): lax.all_to_all(dealt_parts.reshape(devices, capacity, sections * piece_co...]
    all_to_all x0 -> x1, blocking collectives: none -> 57.1 us  [on_device(): lax.all_to_all(dealt, 'col', split_axis=0, concat_axis=0, tiled=True)]
    scatter x2 -> x0, local copies, waits for them, and re-layouts: 37.3 us -> none  [the longest x1 34.4 us: on_device(): recv_index = jnp.zeros((grid_rows,), jnp.int32).at[local_row].set(owner_i...]
    dot_general x2 -> x1, matrix products: 33.3 us -> 0.72 us  [on_device(): lax.dot_general(high, low, (((0,), (0,)), ((), ())), preferred_element_ty...]
    reshape x3 -> x0, local copies, waits for them, and re-layouts: 18.2 us -> none  [the longest x1 9.53 us: on_device(): chosen.reshape(n_row, capacity, sections, n_col, piece_cols)]
    select_n x4 -> x2, other arithmetic: 0.89 us -> 7.01 us  [the longest x1 6.98 us: on_device(): jnp.where(low, (place // 128).astype(jnp.bfloat16)[:, None], zero)]
  transfers between devices with their start and end apart: 5 -> 2, of which waited for: 4 -> 2; matrix products, arithmetic and copies ran while one was open for 13% -> 8% of each run, Pallas kernels for 0% -> 0%
where the time goes in v1:
time: 428 us; the launch traced here: 425 us
  Pallas kernels  216 us (50%)
  waiting for transfers between devices  93.1 us (22%)
  blocking collectives  57.1 us (13%)
  local copies, waits for them, and re-layouts  30 us (7%)
  other arithmetic  14.4 us (3%)
  between operations  13.5 us (3%)
    pallas_call x1, Pallas kernels, spread_multiply(): pl.pallas_call(functools.partial(spread_kernel, lines, width, chunk), out...  216 us
    all_to_all x1, blocking collectives, on_device(): lax.all_to_all(dealt, 'col', split_axis=0, concat_axis=0, tiled=True)  57.1 us
    all_gather x1, waiting for transfers between devices, on_device(): everyone = lax.all_gather(dealt, 'row', axis=0, tiled=False)  47.5 us
    all_gather x1, waiting for transfers between devices, on_device(): vint = lax.all_gather(masked, 'row', axis=1, tiled=True)  45.6 us
    unnamed x4, local copies, waits for them, and re-layouts  12.1 us
    gather x1, local copies, waits for them, and re-layouts, on_device(): everyone.at[found].get(mode='promise_in_bounds')  11.9 us
  transfers between devices with their start and end apart: 2, of which 2 were waited for; matrix products, arithmetic and copies ran while one was open for 8% of the time, Pallas kernels for 0%

profile of v1, /device:TPU:24, one launch (start us, length us, event | category | flops | bytes accessed | tf_op | source)
XLA Modules:
  0.0 425.2 jit_solution(8391270701833009843)
XLA Ops:
  6.5 0.0 all-gather.6.cloned.1.call-start
  6.5 2.7 copy.15
  9.2 0.8 copy.13
  10.0 57.1 %all_to_all.5 = bf16[8,288,512]{2,1,0:T(8,128)(2,1)} all-to-all(bf16[8,288,512]{2,1,0:T(8,128)(2,1)S(1)} %copy.13), channel_id=1, replica_groups=mesh['col'=8,'row'=4] {'col'}, dimensions={0} | all-to-all | bytes 4718592 | tf_op jit(solution)/shard_map/all_to_all | solution.py:216
  67.1 0.0 all-gather.6.cloned.1.call-update
  67.2 0.0 all-gather.4.cloned.1.call-start
  67.2 0.8 dynamic-slice_convert_fusion
  68.0 1.7 mul.81
  69.7 2.8 mul.82
  72.5 0.0 copy-start
  72.5 3.9 mul.83
  76.4 0.0 all-gather.4.cloned.1.call-update
  76.5 0.8 dynamic-slice_convert_fusion.1
  77.2 0.1 copy.14
  77.3 0.1 fusion.22
  77.4 0.0 copy-done
  77.4 0.1 fusion.16
  77.6 7.0 %fusion.5 = (bf16[9216,128]{1,0:T(8,128)(2,1)S(1)}, bf16[9216,128]{1,0:T(8,128)(2,1)S(1)}) fusion(s32[9216]{0:T(1024)S(1)} %get-tuple-element.6, bf16[9216]{0:T(1024)(128)(2,1)S(1)} %get-tuple-element.9, bf16[9216]{0:T(1024)(128)(2,1)S(1)} %fusion.22), kind=kLoop, calls=%fused_computation.7 | loop fusion | flops 3538944 | bytes 4792320 | tf_op jit(solution)/shard_map/jit(_where)/select_n | solution.py:231
  84.5 0.7 fusion.6
  85.3 47.5 %all-gather.6.cloned.1.call-done = bf16[32,288,512]{2,1,0:T(8,128)(2,1)} async-done(((bf16[8,288,512]{2,1,0:T(8,128)(2,1)}), bf16[32,288,512]{2,1,0:T(8,128)(2,1)}) %all-gather.6.cloned.1.call-update) | async-done | bytes 9437200 | tf_op jit(solution)/shard_map/all_gather | solution.py:217
  132.8 11.9 %gather_fusion = bf16[2304,512]{1,0:T(8,128)(2,1)S(1)} fusion(bf16[9216,512]{1,0:T(8,128)(2,1)} %bitcast.19, s32[3072]{0:T(1024)S(1)} %pad_clamp_fusion), kind=kCustom, calls=%fused_computation | custom fusion | bytes 4727808 | tf_op jit(solution)/shard_map/gather | solution.py:245
  144.7 0.7 mul.76
  145.4 1.7 bitcast_multiply_fusion.a_ref
  147.1 45.6 %all-gather.4.cloned.1.call-done = bf16[2,2048,1024]{2,1,0:T(8,128)(2,1)} async-done(((bf16[2,512,1024]{2,1,0:T(8,128)(2,1)}), bf16[2,2048,1024]{2,1,0:T(8,128)(2,1)}) %all-gather.4.cloned.1.call-update) | async-done | bytes 8388624 | tf_op jit(solution)/shard_map/all_gather | solution.py:212
  192.7 216.3 %shard_map.55 = f32[2304,1024]{1,0:T(8,128)} custom-call(bf16[2304,512]{1,0:T(8,128)(2,1)} %bitcast_multiply_fusion.a_ref, bf16[8,512,1024]{2,1,0:T(8,128)(2,1)} %bitcast.24), custom_call_target="tpu_custom_call" | custom-call | flops 19327352832 | bytes 40000000 | tf_op jit(solution)/shard_map/pallas_call | solution.py:161
  409.0 9.4 %copy.21 = f32[2304,1024]{1,0:T(8,128)} copy(f32[2304,1024]{1,0:T(8,128)} %shard_map.55) | data formatting | bytes 18874368
  (3 shorter events, 0.0 us)
Async XLA Ops:
  6.5 126.3 %all-gather.6.cloned.1.call-start = ((), (), s32[]{:S(2)}) async-start(), calls=%async_computation.2 | async-start | bytes 11796480 | tf_op jit(solution)/shard_map/all_gather | solution.py:217
  67.2 125.5 %all-gather.4.cloned.1.call-start = ((), (), s32[]{:S(2)}) async-start(), calls=%async_computation.1 | async-start | bytes 10485760 | tf_op jit(solution)/shard_map/all_gather | solution.py:212
  72.5 4.9 %copy-start = (s32[9216]{0:T(1024)S(1)}, s32[9216]{0:T(1024)}, u32[]{:S(2)}) copy-start(s32[9216]{0:T(1024)} %param.6) | copy-start | bytes 110596
Sparse Core Ops, SparseCore 0:
  67.3 65.4 all-gather.5
  134.4 58.2 all-gather.3

commit v2 on v1

--- a/solution.py
+++ b/solution.py
@@ -20,9 +20,32 @@
 
 
 def spread_kernel(
-    lines, width, chunk, a_ref, b_ref, o_ref, full, load, zsend, zrecv, xsend, xrecv
+    lines,
+    width,
+    n_row,
+    chunk,
+    tile,
+    a_ref,
+    i_ref,
+    m_ref,
+    o_ref,
+    full,
+    b_ref,
+    load,
+    zsend,
+    zrecv,
+    xsend,
+    xrecv,
+    bsend,
+    bcore,
+    brecv,
 ):
     col = lax.axis_index("col")
+    row = lax.axis_index("row")
+    planes = n_row // 2
+    sections, slab_rows, _ = i_ref.shape
+    core = row % 2
+    partner = row + 1 - 2 * core
     z, x = col // width, col % width
     rows = a_ref.shape[0]
     chunks = rows // chunk
@@ -42,8 +65,45 @@
         pl.semaphore_signal(
             barrier, inc=1, device_id={"col": z * width + (x + e) % width}, device_id_type=MESH
         )
+    pl.semaphore_signal(barrier, inc=1, device_id={"row": partner}, device_id_type=MESH)
+    for e in range(1, planes):
+        pl.semaphore_signal(
+            barrier, inc=1, device_id={"row": (row + 2 * e) % n_row}, device_id_type=MESH
+        )
+
+    own = pltpu.make_async_copy(a_ref, full.at[col], load)
+    own.start()
+    tiles = slab_rows // tile
+    for s in range(sections):
+        for i in range(tiles):
+            at = slice(i * tile, (i + 1) * tile)
+            b_ref[s * n_row + row, at, :] = (
+                i_ref[s, at, :] * m_ref[s * tiles + i : s * tiles + i + 1, :]
+            )
     ends = (z == 0).astype(jnp.int32) + (z == lines - 1).astype(jnp.int32)
-    pl.semaphore_wait(barrier, width + 1 - ends)
+    pl.semaphore_wait(barrier, width + 1 - ends + planes)
+    own.wait()
+
+    def sent(s, held, to, sem):
+        k = s * n_row + held
+        return pltpu.make_async_remote_copy(
+            src_ref=b_ref.at[k],
+            dst_ref=b_ref.at[k],
+            send_sem=sem,
+            recv_sem=brecv.at[k],
+            device_id={"row": to},
+            device_id_type=MESH,
+        )
+
+    def beside(s, e):
+        return sent(s, row, (row + 2 * e) % n_row, bsend.at[e - 1, s])
+
+    def inside(s, e):
+        held = (row + 2 * e) % n_row
+        return sent(s, held, partner, bcore.at[e, s])
+
+    def arrival(s, held):
+        return sent(s, held, partner, bcore.at[0, s])
 
     def along(origin, j, side):
         piece = full.at[origin * width + x, pl.ds(pl.multiple_of(j * chunk, chunk), chunk)]
@@ -84,10 +144,6 @@
 
         lax.fori_loop(0, out_cols // 512, part, 0)
 
-    own = pltpu.make_async_copy(a_ref, full.at[col], load)
-    own.start()
-    own.wait()
-
     def step(t, carry):
         d, j = t // chunks, t % chunks
 
@@ -101,7 +157,14 @@
 
             for e in range(1, width):
                 across(z, j, e).start()
-            multiply(col, j, True)
+
+        for s in range(sections):
+
+            @pl.when(t == s)
+            def _(s=s):
+                for e in range(1, planes):
+                    beside(s, e).start()
+                inside(s, 0).start()
 
         for side in (1, -1):
             origin = z - side * d
@@ -116,19 +179,51 @@
 
                 for e in range(1, width):
                     across(origin, j, e).start()
-                multiply(origin * width + x, j)
-
-        for side in (1, -1):
-            origin = z - side * (d - 1)
-            due = (d > 0) if side > 0 else (d > 1)
-
-            @pl.when(due & (origin >= 0) & (origin < lines))
-            def _(origin=origin):
-                for e in range(1, width):
-                    there = (x + e) % width
-                    across(origin, j, e, there).wait_recv()
-                    multiply(origin * width + there, j)
-
+
+        for s in range(sections):
+
+            @pl.when(t == chunks + (s + 1) * chunks // sections - 1)
+            def _(s=s):
+                for e in range(1, planes):
+                    arrival(s, (row + 2 * e) % n_row).wait_recv()
+                    inside(s, e).start()
+
+        @pl.when(t == 2 * chunks)
+        def _():
+            for s in range(sections):
+                for e in range(planes):
+                    arrival(s, (partner + 2 * e) % n_row).wait_recv()
+
+        @pl.when(d == 2)
+        def _():
+            multiply(col, j, True)
+
+        def lagged(apart):
+            for side in (1, -1):
+                origin = z - side * apart
+
+                @pl.when((apart < lines) & (origin >= 0) & (origin < lines))
+                def _(origin=origin):
+                    multiply(origin * width + x, j)
+
+        def crossed(apart):
+            for side in (1, -1):
+                origin = z - side * apart
+                due = True if side > 0 else apart > 0
+
+                @pl.when(due & (origin >= 0) & (origin < lines))
+                def _(origin=origin):
+                    for e in range(1, width):
+                        there = (x + e) % width
+                        across(origin, j, e, there).wait_recv()
+                        multiply(origin * width + there, j)
+
+        def late(i, carry):
+            lagged(i)
+            crossed(i - 1)
+            return carry
+
+        lax.fori_loop(jnp.where(d == 2, 1, d), jnp.where(d < 2, d, d + 1), late, 0)
         return carry
 
     lax.fori_loop(0, (lines + 1) * chunks, step, 0)
@@ -149,30 +244,41 @@
         return carry
 
     lax.fori_loop(0, lines * chunks, drain, 0)
-
-
-def spread_multiply(amp_piece, vint, n_col):
+    for s in range(sections):
+        for e in range(1, planes):
+            beside(s, e).wait_send()
+        for e in range(planes):
+            inside(s, e).wait_send()
+
+
+def spread_multiply(amp_piece, integrals, factors, n_col, n_row, tile):
     lines = 4 if n_col % 4 == 0 else n_col
     width = n_col // lines
     rows, depth = amp_piece.shape
-    out_cols = vint.shape[2]
+    sections, slab_rows, out_cols = integrals.shape
+    planes = n_row // 2
     chunk = 384 if rows % 384 == 0 else rows
     chunks = rows // chunk
     return pl.pallas_call(
-        functools.partial(spread_kernel, lines, width, chunk),
+        functools.partial(spread_kernel, lines, width, n_row, chunk, tile),
         out_shape=jax.ShapeDtypeStruct((rows, out_cols), jnp.float32),
         in_specs=[
             pl.BlockSpec(memory_space=pl.ANY),
+            pl.BlockSpec(memory_space=pltpu.VMEM),
             pl.BlockSpec(memory_space=pltpu.VMEM),
         ],
         out_specs=pl.BlockSpec(memory_space=pltpu.VMEM),
         scratch_shapes=[
             pltpu.VMEM((n_col, rows, depth), jnp.bfloat16),
+            pltpu.VMEM((sections * n_row, slab_rows, out_cols), jnp.bfloat16),
             pltpu.SemaphoreType.DMA,
             pltpu.SemaphoreType.DMA((2, lines, chunks)),
             pltpu.SemaphoreType.DMA((lines, chunks)),
             pltpu.SemaphoreType.DMA((max(width - 1, 1), lines, chunks)),
             pltpu.SemaphoreType.DMA((n_col, chunks)),
+            pltpu.SemaphoreType.DMA((max(planes - 1, 1), sections)),
+            pltpu.SemaphoreType.DMA((planes, sections)),
+            pltpu.SemaphoreType.DMA((sections * n_row,)),
         ],
         compiler_params=pltpu.CompilerParams(
             collective_id=0, has_side_effects=True, vmem_limit_bytes=58 * 1024 * 1024
@@ -180,7 +286,156 @@
         cost_estimate=pl.CostEstimate(
             flops=2 * rows * depth * n_col * out_cols, bytes_accessed=40_000_000, transcendentals=0
         ),
-    )(amp_piece, vint)
+    )(amp_piece, integrals, factors)
+
+
+def deal_kernel(
+    n_row, n_col, tile, a_ref, pair_ref, place_ref, out_ref, found_ref, keep, asend, ysend, csend, recv
+):
+    col = lax.axis_index("col")
+    row = lax.axis_index("row")
+    planes = n_row // 2
+    partner = row + 1 - 2 * (row % 2)
+    _, _, own_rows, width = out_ref.shape
+
+    barrier = pltpu.get_barrier_semaphore()
+    for e in range(1, n_col):
+        pl.semaphore_signal(
+            barrier, inc=1, device_id={"col": (col + e) % n_col}, device_id_type=MESH
+        )
+    pl.semaphore_signal(barrier, inc=1, device_id={"row": partner}, device_id_type=MESH)
+    for e in range(1, planes):
+        pl.semaphore_signal(
+            barrier, inc=1, device_id={"row": (row + 2 * e) % n_row}, device_id_type=MESH
+        )
+    pl.semaphore_wait(barrier, n_col + planes - 1)
+
+    def cut(c):
+        return a_ref.at[:, pl.ds(pl.multiple_of(c * width, width), width)]
+
+    def dealt(e):
+        to = (col + e) % n_col
+        return pltpu.make_async_remote_copy(
+            src_ref=cut(to),
+            dst_ref=out_ref.at[row, col],
+            send_sem=asend.at[e],
+            recv_sem=recv.at[row, col],
+            device_id={"col": to},
+            device_id_type=MESH,
+        )
+
+    def sent(held, c, to, sem, src=None):
+        return pltpu.make_async_remote_copy(
+            src_ref=out_ref.at[held, c] if src is None else src,
+            dst_ref=out_ref.at[held, c],
+            send_sem=sem,
+            recv_sem=recv.at[held, c],
+            device_id={"row": to},
+            device_id_type=MESH,
+        )
+
+    def beside(c, e, src=None):
+        return sent(row, c, (row + 2 * e) % n_row, ysend.at[e - 1, c], src)
+
+    def inside(c, e, src=None):
+        return sent((row + 2 * e) % n_row, c, partner, csend.at[e, c], src)
+
+    mine = pltpu.make_async_copy(cut(col), out_ref.at[row, col], keep)
+    mine.start()
+    for e in range(1, planes):
+        beside(col, e, cut(col)).start()
+
+    def start(e, carry):
+        dealt(e).start()
+        return carry
+
+    lax.fori_loop(1, n_col, start, 0)
+    inside(col, 0, cut(col)).start()
+
+    total = pair_ref.shape[1]
+    tiles = found_ref.shape[0]
+    block = total // 8
+    found_ref[...] = jnp.zeros_like(found_ref)
+
+    def invert(i, carry):
+        at = pl.ds(pl.multiple_of(i * block, block), block)
+        pairs = pair_ref[:, at]
+        here = lax.broadcasted_iota(jnp.int32, (tiles, block), 0) * tile + row * (tiles * tile)
+        high = jnp.where((pairs >= here) & (pairs < here + tile), 1.0, 0.0).astype(jnp.bfloat16)
+        low = (pairs & (tile - 1)) == lax.broadcasted_iota(jnp.int32, (tile, block), 0)
+        for half in range(2):
+            value = jnp.where(low, place_ref[half : half + 1, at], 0.0).astype(jnp.bfloat16)
+            found_ref[:, half * tile : (half + 1) * tile] += lax.dot_general(
+                high, value, (((1,), (1,)), ((), ())), preferred_element_type=jnp.float32
+            )
+        return carry
+
+    lax.fori_loop(0, 8, invert, 0)
+
+    def step(e, carry):
+        @pl.when((e > 0) & (e < n_col))
+        def _():
+            c = (col + n_col - e) % n_col
+            sent(row, c, partner, csend.at[0, c]).wait_recv()
+            for f in range(1, planes):
+                beside(c, f).start()
+            inside(c, 0).start()
+
+        @pl.when(e > 0)
+        def _():
+            c = (col + n_col - (e - 1)) % n_col
+            for f in range(1, planes):
+                sent((row + 2 * f) % n_row, c, partner, csend.at[f, c]).wait_recv()
+                inside(c, f).start()
+
+        return carry
+
+    lax.fori_loop(0, n_col + 1, step, 0)
+    mine.wait()
+
+    def drain(c, carry):
+        for f in range(planes):
+            sent((partner + 2 * f) % n_row, c, partner, csend.at[f, c]).wait_recv()
+            inside(c, f).wait_send()
+        for f in range(1, planes):
+            beside(c, f).wait_send()
+
+        @pl.when(c > 0)
+        def _():
+            dealt(c).wait_send()
+
+        return carry
+
+    lax.fori_loop(0, n_col, drain, 0)
+
+
+def deal(amp_owned, pairs, places, n_row, n_col, tile):
+    own_rows, width_all = amp_owned.shape
+    tiles = pairs.shape[1] // n_row // tile
+    planes = n_row // 2
+    return pl.pallas_call(
+        functools.partial(deal_kernel, n_row, n_col, tile),
+        out_shape=(
+            jax.ShapeDtypeStruct((n_row, n_col, own_rows, width_all // n_col), jnp.bfloat16),
+            jax.ShapeDtypeStruct((tiles, 2 * tile), jnp.float32),
+        ),
+        in_specs=[
+            pl.BlockSpec(memory_space=pl.ANY),
+            pl.BlockSpec(memory_space=pltpu.VMEM),
+            pl.BlockSpec(memory_space=pltpu.VMEM),
+        ],
+        out_specs=(pl.BlockSpec(memory_space=pl.ANY), pl.BlockSpec(memory_space=pltpu.VMEM)),
+        scratch_shapes=[
+            pltpu.SemaphoreType.DMA,
+            pltpu.SemaphoreType.DMA((n_col,)),
+            pltpu.SemaphoreType.DMA((max(planes - 1, 1), n_col)),
+            pltpu.SemaphoreType.DMA((planes, n_col)),
+            pltpu.SemaphoreType.DMA((n_row, n_col)),
+        ],
+        compiler_params=pltpu.CompilerParams(
+            collective_id=1, has_side_effects=True, vmem_limit_bytes=32 * 1024 * 1024
+        ),
+    )(amp_owned, pairs, places)
 
 
 def on_device(amp_owned, pair_of_slot, amp_tiles, integrals, integral_tile_mask):
@@ -204,38 +459,17 @@
         (0, row_at * local_tile_rows, col_at * col_tiles),
         (sections, local_tile_rows, col_tiles),
     )
-    masked = apply_tile_blocks(
-        integrals.reshape(sections * slab_rows, out_cols),
-        tiles_int.reshape(sections * local_tile_rows, col_tiles),
-        tile_size,
-    ).reshape(sections, slab_rows, out_cols)
-    vint = lax.all_gather(masked, "row", axis=1, tiled=True)
-    vint = vint.reshape(n_col, piece_cols, out_cols)
-
-    dealt = amp_owned.reshape(own_rows, n_col, piece_cols).transpose(1, 0, 2)
-    dealt = lax.all_to_all(dealt, "col", split_axis=0, concat_axis=0, tiled=True)
-    everyone = lax.all_gather(dealt, "row", axis=0, tiled=False)
-    everyone = everyone.reshape(total_rows, piece_cols)
+    factors = jnp.repeat(
+        tiles_int.reshape(sections * local_tile_rows, col_tiles).astype(jnp.bfloat16), tile_size, axis=1
+    )
 
     slot = jnp.arange(total_rows, dtype=jnp.int32)
     owner, within = slot // own_rows, slot % own_rows
     place = ((owner % n_row) * n_col + owner // n_row) * own_rows + within
-    high = (
-        (pair_of_slot // tile_size - row_at * row_tiles)[:, None]
-        == jnp.arange(row_tiles, dtype=jnp.int32)[None, :]
-    ).astype(jnp.bfloat16)
-    low = (pair_of_slot % tile_size)[:, None] == jnp.arange(tile_size, dtype=jnp.int32)[None, :]
-    zero = jnp.zeros((), jnp.bfloat16)
-    low = jnp.concatenate(
-        [
-            jnp.where(low, (place // 128).astype(jnp.bfloat16)[:, None], zero),
-            jnp.where(low, (place % 128).astype(jnp.bfloat16)[:, None], zero),
-        ],
-        axis=1,
-    )
-    found = lax.dot_general(
-        high, low, (((0,), (0,)), ((), ())), preferred_element_type=jnp.float32
-    ).astype(jnp.int32)
+    places = jnp.stack([place // 128, place % 128]).astype(jnp.float32)
+    everyone, found = deal(amp_owned, pair_of_slot[None, :], places, n_row, n_col, tile_size)
+    everyone = everyone.reshape(total_rows, piece_cols)
+    found = found.astype(jnp.int32)
     found = (found[:, :tile_size] * 128 + found[:, tile_size:]).reshape(grid_rows)
 
     my_tiles = lax.dynamic_slice(
@@ -244,7 +478,7 @@
     amp_piece = apply_tile_blocks(
         everyone.at[found].get(mode="promise_in_bounds"), my_tiles, tile_size
     )
-    return spread_multiply(amp_piece, vint, n_col)
+    return spread_multiply(amp_piece, integrals, factors, n_col, n_row, tile_size)
 
 
 def solution(mesh):

time: 428 us -> 333 us (0.78)
  waiting for transfers between devices: 93.1 us -> 0 us
  Pallas kernels: 216 us -> 297 us
  blocking collectives: 57.1 us -> 0 us
  between operations: 13.5 us -> 0.06 us
  other arithmetic: 14.4 us -> 5.83 us
    all_gather x2 -> x0, waiting for transfers between devices: 93 us -> none  [the longest x1 47.5 us: on_device(): everyone = lax.all_gather(dealt, 'row', axis=0, tiled=False)]
    pallas_call x1 -> x2, Pallas kernels: 216 us -> 297 us  [the longest x1 214 us: spread_multiply(): pl.pallas_call(functools.partial(spread_kernel, lines, width, n_row, chun...]
    all_to_all x1 -> x0, blocking collectives: 57.1 us -> none  [on_device(): lax.all_to_all(dealt, 'col', split_axis=0, concat_axis=0, tiled=True)]
    select_n x1, other arithmetic: 6.98 us -> 0.65 us  [on_device(): places = jnp.stack([place // 128, place % 128]).astype(jnp.float32)]
    unnamed x4 -> x9, local copies, waits for them, and re-layouts: 12.1 us -> 13.1 us
  transfers between devices with their start and end apart: 2 -> 0, of which waited for: 2 -> 0; matrix products, arithmetic and copies ran while one was open for 8% -> 0% of each run, Pallas kernels for 0% -> 0%
where the time goes in v2:
time: 333 us; the launch traced here: 332 us
  Pallas kernels  297 us (89%)
  local copies, waits for them, and re-layouts  28.7 us (9%)
  other arithmetic  5.83 us (2%)
    pallas_call x1, Pallas kernels, spread_multiply(): pl.pallas_call(functools.partial(spread_kernel, lines, width, n_row, chun...  214 us
    pallas_call x1, Pallas kernels, deal(): pl.pallas_call(functools.partial(deal_kernel, n_row, n_col, tile), out_sh...  83.3 us
    unnamed x9, local copies, waits for them, and re-layouts  13.1 us
    gather x1, local copies, waits for them, and re-layouts, on_device(): everyone.at[found].get(mode='promise_in_bounds')  12.7 us

profile of v2, /device:TPU:24, one launch (start us, length us, event | category | flops | bytes accessed | tf_op | source)
XLA Modules:
  0.0 331.7 jit_solution(12969648219113135503)
XLA Ops:
  0.0 0.0 copy-start.2
  0.0 0.0 copy-start.1
  0.0 0.9 dynamic-slice_convert_fusion.1
  0.9 0.8 dynamic-slice_convert_fusion
  1.7 0.1 copy.7
  1.8 0.1 copy.6
  1.9 0.7 broadcast_bitcast_fusion.m_ref
  2.6 0.7 and_select_fusion
  3.2 0.1 add_convert_fusion.place_ref
  3.3 2.1 mul.72
  5.4 0.0 copy-done.2
  5.4 0.0 copy-done.1
  5.4 83.3 %shard_map.55 = (bf16[4,8,288,512]{3,2,1,0:T(8,128)(2,1)S(1)}, f32[18,256]{1,0:T(8,128)S(1)}) custom-call(bf16[288,4096]{1,0:T(8,128)(2,1)S(1)} %copy-done.1, s32[1,9216]{1,0:T(1,128)S(1)} %bitcast.16, f32[2,9216]{1,0:T(2,128)S(1)} %add_convert_fusion.place_ref), custom_call_target="tpu_custom_call" | custom-call | tf_op jit(solution)/shard_map/pallas_call | solution.py:416
  88.7 0.0 copy-start
  88.7 3.7 %copy-done = bf16[4,8,288,512]{3,2,1,0:T(8,128)(2,1)} copy-done((bf16[4,8,288,512]{3,2,1,0:T(8,128)(2,1)}, bf16[4,8,288,512]{3,2,1,0:T(8,128)(2,1)S(1)}, u32[]{:S(2)}) %copy-start) | copy-done | bytes 9437208
  92.5 0.0 copy-start.3
  92.5 12.7 %gather_fusion = bf16[2304,512]{1,0:T(8,128)(2,1)} fusion(bf16[9216,512]{1,0:T(8,128)(2,1)} %bitcast.15, s32[3072]{0:T(1024)S(1)} %pad_clamp_fusion), kind=kCustom, calls=%fused_computation | custom fusion | bytes 4727808 | tf_op jit(solution)/shard_map/gather | solution.py:479
  105.2 0.0 copy-done.3
  105.2 3.4 %bitcast_multiply_fusion.a_ref = bf16[2304,512]{1,0:T(8,128)(2,1)} fusion(bf16[2304,512]{1,0:T(8,128)(2,1)} %gather_fusion, bf16[288,8,4,128]{3,2,1,0:T(4,128)(2,1)S(1)} %bitcast.17), kind=kLoop, calls=%fused_computation.1 | loop fusion | flops 1179648 | bytes 7077888 | tf_op jit(solution)/shard_map/mul | solution.py:18
  108.6 213.8 %shard_map.56 = f32[2304,1024]{1,0:T(8,128)} custom-call(bf16[2304,512]{1,0:T(8,128)(2,1)} %bitcast_multiply_fusion.a_ref, bf16[2,512,1024]{2,1,0:T(8,128)(2,1)} %i_ref.1, bf16[8,1024]{1,0:T(8,128)(2,1)} %broadcast_bitcast_fusion.m_ref), custom_call_target="tpu_custom_call" | custom-call | flops 19327352832 | bytes 40000000 | tf_op jit(solution)/shard_map/pallas_call | solution.py:262
  322.4 9.4 %copy.13 = f32[2304,1024]{1,0:T(8,128)} copy(f32[2304,1024]{1,0:T(8,128)} %shard_map.56) | data formatting | bytes 18874368
  (4 shorter events, 0.1 us)
Async XLA Ops:
  0.0 5.4 %copy-start.2 = (s32[9216]{0:T(1024)S(1)}, s32[9216]{0:T(1024)}, u32[]{:S(2)}) copy-start(s32[9216]{0:T(1024)} %param.6) | copy-start | bytes 110596
  0.0 5.4 %copy-start.1 = (bf16[288,4096]{1,0:T(8,128)(2,1)S(1)}, bf16[288,4096]{1,0:T(8,128)(2,1)}, u32[]{:S(2)}) copy-start(bf16[288,4096]{1,0:T(8,128)(2,1)} %a_ref.1) | copy-start | bytes 7077892
  88.7 3.7 %copy-start = (bf16[4,8,288,512]{3,2,1,0:T(8,128)(2,1)}, bf16[4,8,288,512]{3,2,1,0:T(8,128)(2,1)S(1)}, u32[]{:S(2)}) copy-start(bf16[4,8,288,512]{3,2,1,0:T(8,128)(2,1)S(1)} %get-tuple-element.7) | copy-start | bytes 28311556
  92.5 12.7 %copy-start.3 = (bf16[18,128,4,128]{3,2,1,0:T(4,128)(2,1)S(1)}, bf16[18,128,4,128]{3,2,1,0:T(4,128)(2,1)}, u32[]{:S(2)}) copy-start(bf16[18,128,4,128]{3,2,1,0:T(4,128)(2,1)} %mul.72) | copy-start | bytes 7077892

commit v3 on v2

--- a/solution.py
+++ b/solution.py
@@ -49,6 +49,8 @@
     z, x = col // width, col % width
     rows = a_ref.shape[0]
     chunks = rows // chunk
+    paired = chunks // 6 if width == 2 else 0
+    beats = chunks + paired
     out_cols = o_ref.shape[1]
 
     barrier = pltpu.get_barrier_semaphore()
@@ -105,13 +107,18 @@
     def arrival(s, held):
         return sent(s, held, partner, bcore.at[0, s])
 
-    def along(origin, j, side):
-        piece = full.at[origin * width + x, pl.ds(pl.multiple_of(j * chunk, chunk), chunk)]
+    def place(origin, v):
+        k = origin * width + jnp.where(v < chunks, x, (x + 1) % width)
+        return k, jnp.where(v < chunks, v, v - chunks)
+
+    def along(origin, v, side):
+        k, j = place(origin, v)
+        piece = full.at[k, pl.ds(pl.multiple_of(j * chunk, chunk), chunk)]
         return pltpu.make_async_remote_copy(
             src_ref=piece,
             dst_ref=piece,
-            send_sem=zsend.at[0 if side > 0 else 1, origin, j],
-            recv_sem=zrecv.at[origin, j],
+            send_sem=zsend.at[0 if side > 0 else 1, origin, v],
+            recv_sem=zrecv.at[origin, v],
             device_id={"col": (z + side) * width + x},
             device_id_type=MESH,
         )
@@ -145,18 +152,26 @@
         lax.fori_loop(0, out_cols // 512, part, 0)
 
     def step(t, carry):
-        d, j = t // chunks, t % chunks
+        d, j = t // beats, t % beats
 
         @pl.when(d == 0)
         def _():
+            @pl.when(j < chunks)
+            def _():
+                for e in range(1, width):
+                    across(z, j, e).start()
+
+            if paired:
+
+                @pl.when(j >= chunks)
+                def _():
+                    across(z, j - chunks, 1, (x + 1) % width).wait_recv()
+
             for side in (1, -1):
 
                 @pl.when((z + side >= 0) & (z + side < lines))
                 def _(side=side):
                     along(z, j, side).start()
-
-            for e in range(1, width):
-                across(z, j, e).start()
 
         for s in range(sections):
 
@@ -177,24 +192,26 @@
                 def _():
                     along(origin, j, side).start()
 
-                for e in range(1, width):
-                    across(origin, j, e).start()
+                @pl.when((j >= paired) & (j < chunks))
+                def _():
+                    for e in range(1, width):
+                        across(origin, j, e).start()
 
         for s in range(sections):
 
-            @pl.when(t == chunks + (s + 1) * chunks // sections - 1)
+            @pl.when(t == beats + (s + 1) * beats // sections - 1)
             def _(s=s):
                 for e in range(1, planes):
                     arrival(s, (row + 2 * e) % n_row).wait_recv()
                     inside(s, e).start()
 
-        @pl.when(t == 2 * chunks)
+        @pl.when(t == 2 * beats)
         def _():
             for s in range(sections):
                 for e in range(planes):
                     arrival(s, (partner + 2 * e) % n_row).wait_recv()
 
-        @pl.when(d == 2)
+        @pl.when((d == 2) & (j < chunks))
         def _():
             multiply(col, j, True)
 
@@ -204,18 +221,23 @@
 
                 @pl.when((apart < lines) & (origin >= 0) & (origin < lines))
                 def _(origin=origin):
-                    multiply(origin * width + x, j)
+                    multiply(*place(origin, j))
 
         def crossed(apart):
             for side in (1, -1):
                 origin = z - side * apart
                 due = True if side > 0 else apart > 0
+                due = due & (j < chunks) & ((apart == 0) | (j >= paired))
 
                 @pl.when(due & (origin >= 0) & (origin < lines))
                 def _(origin=origin):
                     for e in range(1, width):
                         there = (x + e) % width
-                        across(origin, j, e, there).wait_recv()
+
+                        @pl.when(j >= paired)
+                        def _(e=e, there=there):
+                            across(origin, j, e, there).wait_recv()
+
                         multiply(origin * width + there, j)
 
         def late(i, carry):
@@ -226,10 +248,10 @@
         lax.fori_loop(jnp.where(d == 2, 1, d), jnp.where(d < 2, d, d + 1), late, 0)
         return carry
 
-    lax.fori_loop(0, (lines + 1) * chunks, step, 0)
+    lax.fori_loop(0, (lines + 1) * beats, step, 0)
 
     def drain(t, carry):
-        origin, j = t // chunks, t % chunks
+        origin, j = t // beats, t % beats
 
         @pl.when((origin <= z) & (z < lines - 1))
         def _():
@@ -239,11 +261,14 @@
         def _():
             along(origin, j, -1).wait_send()
 
-        for e in range(1, width):
-            across(origin, j, e).wait_send()
+        @pl.when((j < chunks) & ((origin == z) | (j >= paired)))
+        def _():
+            for e in range(1, width):
+                across(origin, j, e).wait_send()
+
         return carry
 
-    lax.fori_loop(0, lines * chunks, drain, 0)
+    lax.fori_loop(0, lines * beats, drain, 0)
     for s in range(sections):
         for e in range(1, planes):
             beside(s, e).wait_send()
@@ -259,6 +284,7 @@
     planes = n_row // 2
     chunk = 384 if rows % 384 == 0 else rows
     chunks = rows // chunk
+    beats = chunks + (chunks // 6 if width == 2 else 0)
     return pl.pallas_call(
         functools.partial(spread_kernel, lines, width, n_row, chunk, tile),
         out_shape=jax.ShapeDtypeStruct((rows, out_cols), jnp.float32),
@@ -272,8 +298,8 @@
             pltpu.VMEM((n_col, rows, depth), jnp.bfloat16),
             pltpu.VMEM((sections * n_row, slab_rows, out_cols), jnp.bfloat16),
             pltpu.SemaphoreType.DMA,
-            pltpu.SemaphoreType.DMA((2, lines, chunks)),
-            pltpu.SemaphoreType.DMA((lines, chunks)),
+            pltpu.SemaphoreType.DMA((2, lines, beats)),
+            pltpu.SemaphoreType.DMA((lines, beats)),
             pltpu.SemaphoreType.DMA((max(width - 1, 1), lines, chunks)),
             pltpu.SemaphoreType.DMA((n_col, chunks)),
             pltpu.SemaphoreType.DMA((max(planes - 1, 1), sections)),

time: 333 us -> 312 us (0.937)
  Pallas kernels: 297 us -> 277 us
    pallas_call x1, Pallas kernels: 214 us -> 193 us  [spread_multiply(): pl.pallas_call(functools.partial(spread_kernel, lines, width, n_row, chun...]
where the time goes in v3:
time: 312 us; the launch traced here: 311 us
  Pallas kernels  277 us (89%)
  local copies, waits for them, and re-layouts  28.7 us (9%)
  other arithmetic  5.83 us (2%)
    pallas_call x1, Pallas kernels, spread_multiply(): pl.pallas_call(functools.partial(spread_kernel, lines, width, n_row, chun...  193 us
    pallas_call x1, Pallas kernels, deal(): pl.pallas_call(functools.partial(deal_kernel, n_row, n_col, tile), out_sh...  83.3 us
    unnamed x9, local copies, waits for them, and re-layouts  13.1 us
    gather x1, local copies, waits for them, and re-layouts, on_device(): everyone.at[found].get(mode='promise_in_bounds')  12.7 us

profile of v3, /device:TPU:24, one launch (start us, length us, event | category | flops | bytes accessed | tf_op | source)
XLA Modules:
  0.0 311.4 jit_solution(13699034042969026168)
XLA Ops:
  0.0 0.0 copy-start.2
  0.0 0.0 copy-start.1
  0.0 0.9 dynamic-slice_convert_fusion.1
  0.9 0.8 dynamic-slice_convert_fusion
  1.7 0.1 copy.7
  1.8 0.1 copy.6
  1.9 0.7 broadcast_bitcast_fusion.m_ref
  2.6 0.7 and_select_fusion
  3.2 0.1 add_convert_fusion.place_ref
  3.3 2.1 mul.72
  5.4 0.0 copy-done.2
  5.4 0.0 copy-done.1
  5.4 83.3 %shard_map.55 = (bf16[4,8,288,512]{3,2,1,0:T(8,128)(2,1)S(1)}, f32[18,256]{1,0:T(8,128)S(1)}) custom-call(bf16[288,4096]{1,0:T(8,128)(2,1)S(1)} %copy-done.1, s32[1,9216]{1,0:T(1,128)S(1)} %bitcast.16, f32[2,9216]{1,0:T(2,128)S(1)} %add_convert_fusion.place_ref), custom_call_target="tpu_custom_call" | custom-call | tf_op jit(solution)/shard_map/pallas_call | solution.py:442
  88.7 0.0 copy-start
  88.7 3.7 %copy-done = bf16[4,8,288,512]{3,2,1,0:T(8,128)(2,1)} copy-done((bf16[4,8,288,512]{3,2,1,0:T(8,128)(2,1)}, bf16[4,8,288,512]{3,2,1,0:T(8,128)(2,1)S(1)}, u32[]{:S(2)}) %copy-start) | copy-done | bytes 9437208
  92.5 0.0 copy-start.3
  92.5 12.7 %gather_fusion = bf16[2304,512]{1,0:T(8,128)(2,1)} fusion(bf16[9216,512]{1,0:T(8,128)(2,1)} %bitcast.15, s32[3072]{0:T(1024)S(1)} %pad_clamp_fusion), kind=kCustom, calls=%fused_computation | custom fusion | bytes 4727808 | tf_op jit(solution)/shard_map/gather | solution.py:505
  105.2 0.0 copy-done.3
  105.2 3.4 %bitcast_multiply_fusion.a_ref = bf16[2304,512]{1,0:T(8,128)(2,1)} fusion(bf16[2304,512]{1,0:T(8,128)(2,1)} %gather_fusion, bf16[288,8,4,128]{3,2,1,0:T(4,128)(2,1)S(1)} %bitcast.17), kind=kLoop, calls=%fused_computation.1 | loop fusion | flops 1179648 | bytes 7077888 | tf_op jit(solution)/shard_map/mul | solution.py:18
  108.6 193.4 %shard_map.56 = f32[2304,1024]{1,0:T(8,128)} custom-call(bf16[2304,512]{1,0:T(8,128)(2,1)} %bitcast_multiply_fusion.a_ref, bf16[2,512,1024]{2,1,0:T(8,128)(2,1)} %i_ref.1, bf16[8,1024]{1,0:T(8,128)(2,1)} %broadcast_bitcast_fusion.m_ref), custom_call_target="tpu_custom_call" | custom-call | flops 19327352832 | bytes 40000000 | tf_op jit(solution)/shard_map/pallas_call | solution.py:288
  302.0 9.4 %copy.13 = f32[2304,1024]{1,0:T(8,128)} copy(f32[2304,1024]{1,0:T(8,128)} %shard_map.56) | data formatting | bytes 18874368
  (4 shorter events, 0.1 us)
Async XLA Ops:
  0.0 5.4 %copy-start.2 = (s32[9216]{0:T(1024)S(1)}, s32[9216]{0:T(1024)}, u32[]{:S(2)}) copy-start(s32[9216]{0:T(1024)} %param.6) | copy-start | bytes 110596
  0.0 5.4 %copy-start.1 = (bf16[288,4096]{1,0:T(8,128)(2,1)S(1)}, bf16[288,4096]{1,0:T(8,128)(2,1)}, u32[]{:S(2)}) copy-start(bf16[288,4096]{1,0:T(8,128)(2,1)} %a_ref.1) | copy-start | bytes 7077892
  88.7 3.7 %copy-start = (bf16[4,8,288,512]{3,2,1,0:T(8,128)(2,1)}, bf16[4,8,288,512]{3,2,1,0:T(8,128)(2,1)S(1)}, u32[]{:S(2)}) copy-start(bf16[4,8,288,512]{3,2,1,0:T(8,128)(2,1)S(1)} %get-tuple-element.7) | copy-start | bytes 28311556
  92.5 12.7 %copy-start.3 = (bf16[18,128,4,128]{3,2,1,0:T(4,128)(2,1)S(1)}, bf16[18,128,4,128]{3,2,1,0:T(4,128)(2,1)}, u32[]{:S(2)}) copy-start(bf16[18,128,4,128]{3,2,1,0:T(4,128)(2,1)} %mul.72) | copy-start | bytes 7077892

commit v4 on v3

--- a/solution.py
+++ b/solution.py
@@ -140,7 +140,7 @@
 
         def part(n, carry):
             cols = pl.ds(pl.multiple_of(n * 512, 512), 512)
-            term = 0.5 * jnp.dot(
+            term = jnp.dot(
                 full[k, at, :], b_ref[k, :, cols], preferred_element_type=jnp.float32
             )
             if first:
@@ -287,7 +287,7 @@
     beats = chunks + (chunks // 6 if width == 2 else 0)
     return pl.pallas_call(
         functools.partial(spread_kernel, lines, width, n_row, chunk, tile),
-        out_shape=jax.ShapeDtypeStruct((rows, out_cols), jnp.float32),
+        out_shape=pltpu.VMEM((rows, out_cols), jnp.float32),
         in_specs=[
             pl.BlockSpec(memory_space=pl.ANY),
             pl.BlockSpec(memory_space=pltpu.VMEM),
@@ -307,7 +307,7 @@
             pltpu.SemaphoreType.DMA((sections * n_row,)),
         ],
         compiler_params=pltpu.CompilerParams(
-            collective_id=0, has_side_effects=True, vmem_limit_bytes=58 * 1024 * 1024
+            collective_id=0, has_side_effects=True, vmem_limit_bytes=44 * 1024 * 1024
         ),
         cost_estimate=pl.CostEstimate(
             flops=2 * rows * depth * n_col * out_cols, bytes_accessed=40_000_000, transcendentals=0
@@ -504,7 +504,7 @@
     amp_piece = apply_tile_blocks(
         everyone.at[found].get(mode="promise_in_bounds"), my_tiles, tile_size
     )
-    return spread_multiply(amp_piece, integrals, factors, n_col, n_row, tile_size)
+    return 0.5 * spread_multiply(amp_piece, integrals, factors, n_col, n_row, tile_size)
 
 
 def solution(mesh):

time: 312 us -> 301 us (0.965)
  local copies, waits for them, and re-layouts: 28.7 us -> 19 us
  Pallas kernels: 277 us -> 273 us
    unnamed x9 -> x6, local copies, waits for them, and re-layouts: 13.1 us -> 6.16 us
    mul x0 -> x1, other arithmetic: none -> 4.86 us  [on_device(): 0.5 * spread_multiply(amp_piece, integrals, factors, n_col, n_row, tile_s...]
    pallas_call x1, Pallas kernels: 193 us -> 190 us  [spread_multiply(): pl.pallas_call(functools.partial(spread_kernel, lines, width, n_row, chun...]
where the time goes in v4:
time: 301 us
  Pallas kernels  273 us (91%)
  local copies, waits for them, and re-layouts  19 us (6%)
  other arithmetic  8.89 us (3%)
    pallas_call x1, Pallas kernels, spread_multiply(): pl.pallas_call(functools.partial(spread_kernel, lines, width, n_row, chun...  190 us
    pallas_call x1, Pallas kernels, deal(): pl.pallas_call(functools.partial(deal_kernel, n_row, n_col, tile), out_sh...  83.3 us
    gather x1, local copies, waits for them, and re-layouts, on_device(): everyone.at[found].get(mode='promise_in_bounds')  11.9 us
    unnamed x6, local copies, waits for them, and re-layouts  6.16 us

profile of v4, /device:TPU:24, one launch (start us, length us, event | category | flops | bytes accessed | tf_op | source)
XLA Modules:
  0.0 301.1 jit_solution(5111358785748986959)
XLA Ops:
  0.0 0.7 and_select_fusion
  0.7 0.1 add_convert_fusion.place_ref
  0.7 0.0 copy-start.1
  0.7 1.7 copy-done.1
  2.4 0.0 copy-start.2
  2.4 0.8 copy-done.2
  3.2 83.3 %shard_map.55 = (bf16[4,8,288,512]{3,2,1,0:T(8,128)(2,1)S(1)}, f32[18,256]{1,0:T(8,128)S(1)}) custom-call(bf16[288,4096]{1,0:T(8,128)(2,1)S(1)} %copy-done.1, s32[1,9216]{1,0:T(1,128)S(1)} %bitcast.16, f32[2,9216]{1,0:T(2,128)S(1)} %add_convert_fusion.place_ref), custom_call_target="tpu_custom_call" | custom-call | tf_op jit(solution)/shard_map/pallas_call | solution.py:442
  86.5 0.0 copy-start
  86.5 3.7 %copy-done = bf16[4,8,288,512]{3,2,1,0:T(8,128)(2,1)} copy-done((bf16[4,8,288,512]{3,2,1,0:T(8,128)(2,1)}, bf16[4,8,288,512]{3,2,1,0:T(8,128)(2,1)S(1)}, u32[]{:S(2)}) %copy-start) | copy-done | bytes 9437208
  90.3 11.9 %gather_fusion = bf16[2304,512]{1,0:T(8,128)(2,1)S(1)} fusion(bf16[9216,512]{1,0:T(8,128)(2,1)} %bitcast.15, s32[3072]{0:T(1024)S(1)} %pad_clamp_fusion), kind=kCustom, calls=%fused_computation | custom fusion | bytes 4727808 | tf_op jit(solution)/shard_map/gather | solution.py:505
  102.3 0.8 dynamic-slice_convert_fusion.1
  103.0 0.1 copy.6
  103.1 0.7 mul.78
  103.8 1.7 bitcast_multiply_fusion.a_ref
  105.5 0.8 dynamic-slice_convert_fusion
  106.3 0.1 copy.7
  106.4 0.1 broadcast_bitcast_fusion.m_ref
  106.5 189.8 %shard_map.56 = f32[2304,1024]{1,0:T(8,128)S(1)} custom-call(bf16[2304,512]{1,0:T(8,128)(2,1)} %bitcast_multiply_fusion.a_ref, bf16[2,512,1024]{2,1,0:T(8,128)(2,1)} %i_ref.1, bf16[8,1024]{1,0:T(8,128)(2,1)S(1)} %broadcast_bitcast_fusion.m_ref), custom_call_target="tpu_custom_call" | custom-call | flops 19327352832 | bytes 40000000 | tf_op jit(solution)/shard_map/pallas_call | solution.py:288
  296.3 4.9 %broadcast_multiply_fusion = f32[2304,1024]{1,0:T(8,128)} fusion(f32[2304,1024]{1,0:T(8,128)S(1)} %shard_map.56), kind=kLoop, calls=%fused_computation.1 | loop fusion | flops 2359296 | bytes 18874368 | tf_op jit(solution)/shard_map/mul | solution.py:507
  (4 shorter events, 0.1 us)
Async XLA Ops:
  0.7 1.7 copy-start.1
  2.4 0.8 copy-start.2
  86.5 3.7 %copy-start = (bf16[4,8,288,512]{3,2,1,0:T(8,128)(2,1)}, bf16[4,8,288,512]{3,2,1,0:T(8,128)(2,1)S(1)}, u32[]{:S(2)}) copy-start(bf16[4,8,288,512]{3,2,1,0:T(8,128)(2,1)S(1)} %get-tuple-element.7) | copy-start | bytes 28311556

commit v5 on v4

--- a/solution.py
+++ b/solution.py
@@ -282,7 +282,7 @@
     rows, depth = amp_piece.shape
     sections, slab_rows, out_cols = integrals.shape
     planes = n_row // 2
-    chunk = 384 if rows % 384 == 0 else rows
+    chunk = 192 if rows % 192 == 0 else rows
     chunks = rows // chunk
     beats = chunks + (chunks // 6 if width == 2 else 0)
     return pl.pallas_call(
@@ -442,15 +442,15 @@
     return pl.pallas_call(
         functools.partial(deal_kernel, n_row, n_col, tile),
         out_shape=(
-            jax.ShapeDtypeStruct((n_row, n_col, own_rows, width_all // n_col), jnp.bfloat16),
+            pltpu.HBM((n_row, n_col, own_rows, width_all // n_col), jnp.bfloat16),
             jax.ShapeDtypeStruct((tiles, 2 * tile), jnp.float32),
         ),
         in_specs=[
-            pl.BlockSpec(memory_space=pl.ANY),
+            pl.BlockSpec(memory_space=pltpu.HBM),
             pl.BlockSpec(memory_space=pltpu.VMEM),
             pl.BlockSpec(memory_space=pltpu.VMEM),
         ],
-        out_specs=(pl.BlockSpec(memory_space=pl.ANY), pl.BlockSpec(memory_space=pltpu.VMEM)),
+        out_specs=(pl.BlockSpec(memory_space=pltpu.HBM), pl.BlockSpec(memory_space=pltpu.VMEM)),
         scratch_shapes=[
             pltpu.SemaphoreType.DMA,
             pltpu.SemaphoreType.DMA((n_col,)),

time: 301 us -> 304 us (level)
  Pallas kernels: 273 us -> 279 us
  local copies, waits for them, and re-layouts: 19 us -> 15.3 us
    pallas_call x1, Pallas kernels: 190 us -> 195 us  [spread_multiply(): pl.pallas_call(functools.partial(spread_kernel, lines, width, n_row, chun...]
    unnamed x6 -> x4, local copies, waits for them, and re-layouts: 6.16 us -> 2.43 us
where the time goes in v5:
time: 304 us; the launch traced here: 303 us
  Pallas kernels  279 us (92%)
  local copies, waits for them, and re-layouts  15.3 us (5%)
  other arithmetic  8.88 us (3%)
    pallas_call x1, Pallas kernels, spread_multiply(): pl.pallas_call(functools.partial(spread_kernel, lines, width, n_row, chun...  195 us
    pallas_call x1, Pallas kernels, deal(): pl.pallas_call(functools.partial(deal_kernel, n_row, n_col, tile), out_sh...  84.1 us
    gather x1, local copies, waits for them, and re-layouts, on_device(): everyone.at[found].get(mode='promise_in_bounds')  11.9 us

profile of v5, /device:TPU:24, one launch (start us, length us, event | category | flops | bytes accessed | tf_op | source)
XLA Modules:
  0.0 303.2 jit_solution(14386094143518027)
XLA Ops:
  0.0 0.7 and_select_fusion
  0.7 0.1 add_convert_fusion.place_ref
  0.7 0.0 copy-start
  0.7 1.7 copy-done
  2.4 0.0 copy-start.1
  2.4 0.8 copy-done.1
  3.2 84.1 %shard_map.55 = (bf16[4,8,288,512]{3,2,1,0:T(8,128)(2,1)}, f32[18,256]{1,0:T(8,128)S(1)}) custom-call(bf16[288,4096]{1,0:T(8,128)(2,1)S(1)} %copy-done, s32[1,9216]{1,0:T(1,128)S(1)} %bitcast.15, f32[2,9216]{1,0:T(2,128)S(1)} %add_convert_fusion.place_ref), custom_call_target="tpu_custom_call" | custom-call | tf_op jit(solution)/shard_map/pallas_call | solution.py:442
  87.3 11.9 %gather_fusion = bf16[2304,512]{1,0:T(8,128)(2,1)S(1)} fusion(bf16[9216,512]{1,0:T(8,128)(2,1)} %bitcast.16, s32[3072]{0:T(1024)S(1)} %pad_clamp_fusion), kind=kCustom, calls=%fused_computation | custom fusion | bytes 4727808 | tf_op jit(solution)/shard_map/gather | solution.py:505
  99.2 0.8 dynamic-slice_convert_fusion.1
  100.0 0.1 copy.6
  100.1 0.7 mul.78
  100.8 1.7 bitcast_multiply_fusion.a_ref
  102.5 0.8 dynamic-slice_convert_fusion
  103.3 0.1 copy.7
  103.4 0.1 broadcast_bitcast_fusion.m_ref
  103.5 194.8 %shard_map.56 = f32[2304,1024]{1,0:T(8,128)S(1)} custom-call(bf16[2304,512]{1,0:T(8,128)(2,1)} %bitcast_multiply_fusion.a_ref, bf16[2,512,1024]{2,1,0:T(8,128)(2,1)} %i_ref.1, bf16[8,1024]{1,0:T(8,128)(2,1)S(1)} %broadcast_bitcast_fusion.m_ref), custom_call_target="tpu_custom_call" | custom-call | flops 19327352832 | bytes 40000000 | tf_op jit(solution)/shard_map/pallas_call | solution.py:288
  298.3 4.9 %broadcast_multiply_fusion = f32[2304,1024]{1,0:T(8,128)} fusion(f32[2304,1024]{1,0:T(8,128)S(1)} %shard_map.56), kind=kLoop, calls=%fused_computation.1 | loop fusion | flops 2359296 | bytes 18874368 | tf_op jit(solution)/shard_map/mul | solution.py:507
  (4 shorter events, 0.1 us)
Async XLA Ops:
  0.7 1.7 copy-start
  2.4 0.8 copy-start.1

commit v6 on v5

--- a/solution.py
+++ b/solution.py
@@ -76,12 +76,6 @@
     own = pltpu.make_async_copy(a_ref, full.at[col], load)
     own.start()
     tiles = slab_rows // tile
-    for s in range(sections):
-        for i in range(tiles):
-            at = slice(i * tile, (i + 1) * tile)
-            b_ref[s * n_row + row, at, :] = (
-                i_ref[s, at, :] * m_ref[s * tiles + i : s * tiles + i + 1, :]
-            )
     ends = (z == 0).astype(jnp.int32) + (z == lines - 1).astype(jnp.int32)
     pl.semaphore_wait(barrier, width + 1 - ends + planes)
     own.wait()
@@ -177,6 +171,11 @@
 
             @pl.when(t == s)
             def _(s=s):
+                for i in range(tiles):
+                    at = slice(i * tile, (i + 1) * tile)
+                    b_ref[s * n_row + row, at, :] = (
+                        i_ref[s, at, :] * m_ref[s * tiles + i : s * tiles + i + 1, :]
+                    )
                 for e in range(1, planes):
                     beside(s, e).start()
                 inside(s, 0).start()
@@ -282,7 +281,7 @@
     rows, depth = amp_piece.shape
     sections, slab_rows, out_cols = integrals.shape
     planes = n_row // 2
-    chunk = 192 if rows % 192 == 0 else rows
+    chunk = 384 if rows % 384 == 0 else rows
     chunks = rows // chunk
     beats = chunks + (chunks // 6 if width == 2 else 0)
     return pl.pallas_call(

time: 304 us -> 298 us (0.980)
  Pallas kernels: 279 us -> 274 us
    pallas_call x1, Pallas kernels: 195 us -> 190 us  [spread_multiply(): pl.pallas_call(functools.partial(spread_kernel, lines, width, n_row, chun...]
where the time goes in v6:
time: 298 us
  Pallas kernels  274 us (92%)
  local copies, waits for them, and re-layouts  15.3 us (5%)
  other arithmetic  8.88 us (3%)
    pallas_call x1, Pallas kernels, spread_multiply(): pl.pallas_call(functools.partial(spread_kernel, lines, width, n_row, chun...  190 us
    pallas_call x1, Pallas kernels, deal(): pl.pallas_call(functools.partial(deal_kernel, n_row, n_col, tile), out_sh...  84.1 us
    gather x1, local copies, waits for them, and re-layouts, on_device(): everyone.at[found].get(mode='promise_in_bounds')  11.9 us

profile of v6, /device:TPU:24, one launch (start us, length us, event | category | flops | bytes accessed | tf_op | source)
XLA Modules:
  0.0 297.9 jit_solution(17463781539609491731)
XLA Ops:
  0.0 0.7 and_select_fusion
  0.7 0.1 add_convert_fusion.place_ref
  0.7 0.0 copy-start
  0.7 1.7 copy-done
  2.4 0.0 copy-start.1
  2.4 0.8 copy-done.1
  3.2 84.1 %shard_map.55 = (bf16[4,8,288,512]{3,2,1,0:T(8,128)(2,1)}, f32[18,256]{1,0:T(8,128)S(1)}) custom-call(bf16[288,4096]{1,0:T(8,128)(2,1)S(1)} %copy-done, s32[1,9216]{1,0:T(1,128)S(1)} %bitcast.15, f32[2,9216]{1,0:T(2,128)S(1)} %add_convert_fusion.place_ref), custom_call_target="tpu_custom_call" | custom-call | tf_op jit(solution)/shard_map/pallas_call | solution.py:441
  87.3 11.9 %gather_fusion = bf16[2304,512]{1,0:T(8,128)(2,1)S(1)} fusion(bf16[9216,512]{1,0:T(8,128)(2,1)} %bitcast.16, s32[3072]{0:T(1024)S(1)} %pad_clamp_fusion), kind=kCustom, calls=%fused_computation | custom fusion | bytes 4727808 | tf_op jit(solution)/shard_map/gather | solution.py:504
  99.2 0.8 dynamic-slice_convert_fusion.1
  100.0 0.1 copy.6
  100.1 0.7 mul.78
  100.8 1.7 bitcast_multiply_fusion.a_ref
  102.5 0.8 dynamic-slice_convert_fusion
  103.3 0.1 copy.7
  103.4 0.1 broadcast_bitcast_fusion.m_ref
  103.5 189.6 %shard_map.56 = f32[2304,1024]{1,0:T(8,128)S(1)} custom-call(bf16[2304,512]{1,0:T(8,128)(2,1)} %bitcast_multiply_fusion.a_ref, bf16[2,512,1024]{2,1,0:T(8,128)(2,1)} %i_ref.1, bf16[8,1024]{1,0:T(8,128)(2,1)S(1)} %broadcast_bitcast_fusion.m_ref), custom_call_target="tpu_custom_call" | custom-call | flops 19327352832 | bytes 40000000 | tf_op jit(solution)/shard_map/pallas_call | solution.py:287
  293.1 4.9 %broadcast_multiply_fusion = f32[2304,1024]{1,0:T(8,128)} fusion(f32[2304,1024]{1,0:T(8,128)S(1)} %shard_map.56), kind=kLoop, calls=%fused_computation.1 | loop fusion | flops 2359296 | bytes 18874368 | tf_op jit(solution)/shard_map/mul | solution.py:506
  (4 shorter events, 0.1 us)
Async XLA Ops:
  0.7 1.7 copy-start
  2.4 0.8 copy-start.1
